TPU v7x, 32 devices: a whole 2x2x4 slice. The times are simulated.
32 devices in a mesh: groups: 2 (over y), afd: 4 (over z), tp: 4 (over x, core).
Axes of the slice: x: 2, y: 2, z: 4, core: 2. Of those that a mesh axis runs over, the one named last changes fastest.
Arguments:
- queries: bfloat16 [16, 64, 128], P(('groups', 'afd'), 'tp'), parts along dimension 0, may hold values from -27 to 27
- cache_keys: bfloat16 [16, 4, 256, 128], P(('groups', 'afd'), 'tp'), parts along dimension 0, may hold values from -4 to 4
- cache_values: bfloat16 [16, 4, 256, 128], P(('groups', 'afd'), 'tp'), parts along dimension 0, may hold values from -6 to 6
- new_keys: bfloat16 [16, 4, 128], P(('groups', 'afd'), 'tp'), parts along dimension 0, may hold values from -4 to 4
- new_values: bfloat16 [16, 4, 128], P(('groups', 'afd'), 'tp'), parts along dimension 0, may hold values from -6 to 6
- cache_lengths: int32 [16], P(('groups', 'afd')), parts along dimension 0, may hold values from 1 to 256, as said below
- moe_in: bfloat16 [384, 4096], P(('groups', 'afd'), 'tp'), parts along dimension 0, may hold values from -6 to 6
- expert_ids: int32 [384, 8], P(('groups', 'afd')), parts along dimension 0, may hold values from 0 to 63, all different within a row; in each aligned block of 48 rows (0 to 47, 48 to 95, ...) at most 9 rows name the same one
- gate_index: int32 [384, 8], P(('groups', 'afd')), parts along dimension 0, may hold values from 0 to 255
- gate_table: float32 [256], replicated, may hold values from 0.05 to 1
- gate_weight: bfloat16 [64, 4096, 768], P('afd', None, 'tp'), may hold values from -0.09375 to 0.09375
- up_weight: bfloat16 [64, 4096, 768], P('afd', None, 'tp'), may hold values from -0.09375 to 0.09375
- down_weight: bfloat16 [64, 768, 4096], P('afd', 'tp'), may hold values from -0.21875 to 0.21875
Outputs:
- attn_out: bfloat16 [16, 64, 128], P(('groups', 'afd'), 'tp'), parts along dimension 0
- moe_out: bfloat16 [384, 4096], P(('groups', 'afd'), 'tp'), parts along dimension 0
There are 2 independent parts, one for each index of `groups`. A program takes and returns all parts, laid end to end along the dimension named above; an argument that names none is the same for every part. Nothing has to cross between parts.
Inputs may be any that keep to these rules, and one draw needn't show every extreme that they name: `expert_ids`: among the 48 tokens of one index of afd, no expert is chosen more than 9 times, and in every draw some expert is chosen exactly 9 times there; each token names 8 different experts. `cache_lengths`: some request has all 256 positions valid.
All inputs are finite; a program needn't handle non-finite values.
Results may differ from a plain program's by a relative error of at most 0.013.
Values may be sent and summed in bfloat16 or wider, within the bound.
A program may use at most 192 MiB of HBM per device.

v0:
```python
import math

import jax
import jax.numpy as jnp
from jax import lax
from jax.sharding import PartitionSpec as P

EXPERTS = 64
CAP = 9


def attend(queries, cache_keys, cache_values, new_keys, new_values, cache_lengths):
    requests, head_count, head_width = queries.shape
    kv_heads = cache_keys.shape[1]
    grouped = queries.reshape(requests, kv_heads, head_count // kv_heads, head_width)
    score_scale = 1.0 / math.sqrt(head_width)
    scores = (
        jnp.einsum("rkgd,rkld->rkgl", grouped, cache_keys, preferred_element_type=jnp.float32)
        * score_scale
    )
    fresh = (
        jnp.einsum("rkgd,rkd->rkg", grouped, new_keys, preferred_element_type=jnp.float32)
        * score_scale
    )
    positions = jnp.arange(cache_keys.shape[2], dtype=jnp.int32)
    valid = positions[None, None, None, :] < cache_lengths[:, None, None, None]
    masked = jnp.where(valid, scores, -jnp.inf)
    largest = jnp.maximum(jnp.max(masked, axis=3), fresh)
    exp_scores = jnp.where(valid, jnp.exp(masked - largest[..., None]), 0.0)
    fresh_prob = jnp.exp(fresh - largest)
    denominator = jnp.sum(exp_scores, axis=3) + fresh_prob
    weights = (exp_scores / denominator[..., None]).astype(jnp.bfloat16)
    fresh_weight = (fresh_prob / denominator).astype(jnp.bfloat16)
    mixed = jnp.einsum("rkgl,rkld->rkgd", weights, cache_values, preferred_element_type=jnp.float32)
    mixed = (
        mixed
        + fresh_weight.astype(jnp.float32)[..., None]
        * new_values.astype(jnp.float32)[:, :, None, :]
    )
    return mixed.reshape(requests, head_count, head_width).astype(jnp.bfloat16)


def ranks(choice_ids):
    flat_ids = choice_ids.reshape(-1)
    matches = (flat_ids[:, None] == jnp.arange(EXPERTS, dtype=jnp.int32)[None, :]).astype(jnp.int32)
    earlier = jnp.cumsum(matches, axis=0) - matches
    return jnp.sum(earlier * matches, axis=1).reshape(choice_ids.shape)


def on_device(
    queries,
    cache_keys,
    cache_values,
    new_keys,
    new_values,
    cache_lengths,
    moe_in,
    expert_ids,
    gate_index,
    gate_table,
    gate_weight,
    up_weight,
    down_weight,
):
    attn_out = attend(queries, cache_keys, cache_values, new_keys, new_values, cache_lengths)
    owners = lax.axis_size("afd")
    held_experts = gate_weight.shape[0]
    slot_id = expert_ids * CAP + ranks(expert_ids)
    slot_count = owners * held_experts * CAP
    slot_index = jnp.arange(slot_count, dtype=jnp.int32)[:, None, None]
    placing = jnp.any(slot_index == slot_id[None], axis=2).astype(jnp.bfloat16)
    whole_rows = lax.all_gather(moe_in, "tp", axis=1, tiled=True)
    sending = jnp.dot(placing, whole_rows, preferred_element_type=jnp.float32).astype(jnp.bfloat16)
    sending = sending.reshape(owners, held_experts, CAP, whole_rows.shape[1])
    received = lax.all_to_all(sending, "afd", split_axis=0, concat_axis=0, tiled=True)
    gate_part = jnp.einsum(
        "snce,nef->sncf", received, gate_weight, preferred_element_type=jnp.float32
    )
    up_part = jnp.einsum("snce,nef->sncf", received, up_weight, preferred_element_type=jnp.float32)
    hidden = (jax.nn.silu(gate_part) * up_part).astype(jnp.bfloat16)
    partial_value = jnp.einsum(
        "sncf,nfd->sncd", hidden, down_weight, preferred_element_type=jnp.float32
    )
    summed = lax.psum_scatter(
        partial_value.astype(jnp.bfloat16), "tp", scatter_dimension=3, tiled=True
    )
    answers = lax.all_to_all(summed, "afd", split_axis=0, concat_axis=0, tiled=True)
    returned_rows = answers.reshape(slot_count, answers.shape[3])
    picked = jnp.take(returned_rows, slot_id, axis=0).astype(jnp.float32)
    table_hits = (
        gate_index[..., None] == jnp.arange(gate_table.shape[0], dtype=jnp.int32)[None, None, :]
    ).astype(jnp.float32)
    raw_gates = jnp.sum(table_hits * gate_table[None, None, :], axis=2)
    route_weight = raw_gates / jnp.sum(raw_gates, axis=1, keepdims=True)
    moe_out = jnp.einsum("tk,tkd->td", route_weight, picked).astype(jnp.bfloat16)
    return (attn_out, moe_out)


def solution(mesh):
    placed = (
        P(("groups", "afd"), "tp", None),
        P(("groups", "afd"), "tp", None, None),
        P(("groups", "afd"), "tp", None, None),
        P(("groups", "afd"), "tp", None),
        P(("groups", "afd"), "tp", None),
        P(("groups", "afd")),
        P(("groups", "afd"), "tp"),
        P(("groups", "afd"), None),
        P(("groups", "afd"), None),
        P(),
        P("afd", None, "tp"),
        P("afd", None, "tp"),
        P("afd", "tp", None),
    )
    return jax.shard_map(
        on_device,
        mesh=mesh,
        in_specs=placed,
        out_specs=(P(("groups", "afd"), "tp", None), P(("groups", "afd"), "tp")),
        check_vma=False,
    )
```

profile of v0, /device:TPU:0, one launch (start us, length us, event | category | flops | bytes accessed | tf_op | source)
XLA Modules:
  0.0 309.0 jit_solution(1219987013247427314)
XLA Ops:
  7.2 0.0 copy-start
  7.2 0.0 reduce-scatter.2.cloned.1.call-start
  7.2 0.8 copy.50
  8.0 0.1 eq.58
  8.1 0.1 eq.54
  8.2 0.9 reduce-window.6
  9.1 0.2 slice_reduce_fusion
  9.4 0.1 fusion.40
  9.5 0.1 reshape.126
  9.6 0.1 copy.53
  9.7 0.7 compare_and_fusion
  10.4 0.1 copy.55
  10.5 0.4 fusion.32
  10.8 8.1 %all_gather.3 = bf16[48,4096]{1,0:T(8,128)(2,1)S(1)} all-gather(bf16[48,1024]{1,0:T(8,128)(2,1)} %param.19), channel_id=1, replica_groups=mesh['groups'=2,'afd'=4,'tp'=4] {'tp'}, dimensions={1}, use_global_device_ids=true | all-gather | bytes 491520 | tf_op jit(solution)/shard_map/all_gather | solution.py:72
  19.0 3.6 %convolution_convert_fusion = bf16[576,4096]{1,0:T(8,128)(2,1)} fusion(pred[576,48]{0,1:T(8,128)(4,1)S(1)} %fusion.32, bf16[48,4096]{1,0:T(8,128)(2,1)S(1)} %all_gather.3), kind=kOutput, calls=%fused_computation.10 | convolution fusion | flops 228851712 | bytes 5139456 | tf_op jit(solution)/shard_map/dot_general | solution.py:73
  22.5 8.1 %reshape.127 = bf16[4,16,9,4096]{3,2,1,0:T(8,128)(2,1)} reshape(bf16[576,4096]{1,0:T(8,128)(2,1)} %convolution_convert_fusion) | data formatting | bytes 9437184 | tf_op jit(solution)/shard_map/reshape | solution.py:74
  30.6 6.2 %copy.56 = bf16[4,16,9,4096]{3,1,2,0:T(8,128)(2,1)S(1)} copy(bf16[4,16,9,4096]{3,2,1,0:T(8,128)(2,1)} %reshape.127) | data formatting | bytes 9437184 | tf_op jit(solution)/shard_map/reshape | solution.py:74
  36.9 109.7 %all_to_all.10 = bf16[4,16,9,4096]{3,1,2,0:T(8,128)(2,1)} all-to-all(bf16[4,16,9,4096]{3,1,2,0:T(8,128)(2,1)S(1)} %copy.56), channel_id=1, replica_groups=mesh['groups'=2,'afd'=4,'tp'=4] {'afd'}, dimensions={0} | all-to-all | bytes 9437184 | tf_op jit(solution)/shard_map/all_to_all | solution.py:75
  146.5 13.7 %fusion.10 = f32[4,16,9,192]{3,2,0,1:T(8,128)S(1)} fusion(bf16[16,4096,192]{1,2,0:T(8,128)(2,1)} %param.23, bf16[4,16,9,4096]{3,1,2,0:T(8,128)(2,1)} %all_to_all.10), kind=kOutput, calls=%fused_computation.11 | convolution fusion | flops 905969664 | bytes 30326784 | tf_op jit(solution)/shard_map/snce,nef->sncf/dot_general | solution.py:76
  160.2 14.0 %fusion.25 = bf16[4,16,9,192]{3,2,0,1:T(8,128)(2,1)S(1)} fusion(bf16[16,4096,192]{1,2,0:T(8,128)(2,1)} %param.24, bf16[4,16,9,4096]{3,1,2,0:T(8,128)(2,1)} %all_to_all.10, f32[4,16,9,192]{3,2,0,1:T(8,128)S(1)} %fusion.10), kind=kOutput, calls=%fused_computation.14 | convolution fusion | flops 906633216 | bytes 30547968 | tf_op jit(solution)/shard_map/snce,nef->sncf/dot_general | solution.py:79
  174.2 16.2 %convert_bitcast_fusion = bf16[4,16,9,4096]{3,2,0,1:T(8,128)(2,1)} fusion(bf16[4,16,9,192]{3,2,0,1:T(8,128)(2,1)S(1)} %fusion.25, bf16[16,192,4096]{2,1,0:T(8,128)(2,1)} %param.25), kind=kOutput, calls=%fused_computation.9 | convolution fusion | flops 908328960 | bytes 30105600 | tf_op jit(solution)/shard_map/sncf,nfd->sncd/dot_general | solution.py:81
  190.4 0.0 copy-start.3
  190.4 0.0 copy-start.7
  190.4 0.0 copy-start.4
  190.4 0.0 reduce-scatter.2.cloned.1.call-update
  190.5 0.1 copy.61
  190.6 0.1 reshape.132
  190.6 0.1 copy.54
  190.7 0.3 copy-done.2
  191.1 0.1 copy.49
  191.2 0.0 copy-done.5
  191.2 0.1 fusion.47
  191.3 69.8 %reduce-scatter.2.cloned.1.call-done = bf16[4,16,9,1024]{3,2,0,1:T(8,128)(2,1)} async-done(((bf16[4,16,9,4096]{3,2,0,1:T(8,128)(2,1)}), bf16[4,16,9,1024]{3,2,0,1:T(8,128)(2,1)}) %reduce-scatter.2.cloned.1.call-update) | async-done | bytes 1179664 | tf_op jit(solution)/shard_map/reduce_scatter | solution.py:84
  261.1 3.3 %copy.59 = bf16[4,16,9,1024]{3,1,2,0:T(8,128)(2,1)} copy(bf16[4,16,9,1024]{3,2,0,1:T(8,128)(2,1)} %reduce-scatter.2.cloned.1.call-done) | data formatting | bytes 2359296 | tf_op jit(solution)/shard_map/reduce_scatter | solution.py:84
  264.4 4.6 %all-to-all-start.1 = ((bf16[4,16,9,1024]{3,1,2,0:T(8,128)(2,1)}), bf16[4,16,9,1024]{3,1,2,0:T(8,128)(2,1)S(1)}, u32[]{:S(2)}, u32[]{:S(2)}) async-start(bf16[4,16,9,1024]{3,1,2,0:T(8,128)(2,1)} %copy.59), calls=%async_computation.2 | async-start | bytes 2359296 | tf_op jit(solution)/shard_map/all_to_all | solution.py:87
  269.1 0.1 iota_compare_fusion.4
  269.1 0.0 copy-done
  269.1 0.2 fusion.53
  269.4 0.2 fusion.42
  269.5 0.8 select_reduce_fusion
  270.4 0.1 broadcast_divide_fusion
  270.5 0.8 fusion.31
  271.3 26.3 %all-to-all-done.1 = bf16[4,16,9,1024]{3,1,2,0:T(8,128)(2,1)S(1)} async-done(((bf16[4,16,9,1024]{3,1,2,0:T(8,128)(2,1)}), bf16[4,16,9,1024]{3,1,2,0:T(8,128)(2,1)S(1)}, u32[]{:S(2)}, u32[]{:S(2)}) %all-to-all-start.1) | async-done | bytes 1179680 | tf_op jit(solution)/shard_map/all_to_all | solution.py:87
  297.6 0.8 copy.60
  298.4 0.6 reshape.128
  298.9 2.1 gather_fusion
  301.0 0.4 fusion.33
  301.4 0.7 copy.86
  (16 shorter events, 0.1 us)
Async XLA Ops:
  7.2 262.0 %copy-start = (bf16[2,1,256,128]{3,2,1,0:T(8,128)(2,1)S(1)}, bf16[2,1,256,128]{3,2,1,0:T(8,128)(2,1)}, u32[]{:S(2)}) copy-start(bf16[2,1,256,128]{3,2,1,0:T(8,128)(2,1)} %param.14) | copy-start | bytes 393220
  7.2 253.9 %reduce-scatter.2.cloned.1.call-start = ((), (), s32[]{:S(2)}) async-start(), calls=%async_computation.3 | async-start | bytes 10485760 | tf_op jit(solution)/shard_map/reduce_scatter | solution.py:84
  190.4 0.7 copy-start.2
  190.4 0.8 copy-start.1
  190.4 0.8 copy-start.5
  190.4 78.7 %copy-start.6 = (s32[2]{0:T(128)S(1)}, s32[2]{0:T(128)}, u32[]{:S(2)}) copy-start(s32[2]{0:T(128)} %param.18) | copy-start | bytes 28
  190.4 79.1 %copy-start.3 = (f32[256]{0:T(256)S(1)}, f32[256]{0:T(256)}, u32[]{:S(2)}) copy-start(f32[256]{0:T(256)} %param.22) | copy-start | bytes 3076
  190.4 79.9 %copy-start.7 = (bf16[2,1,128]{2,0,1:T(2,128)(2,1)S(1)}, bf16[2,1,128]{2,0,1:T(2,128)(2,1)}, u32[]{:S(2)}) copy-start(bf16[2,1,128]{2,0,1:T(2,128)(2,1)} %param.17) | copy-start | bytes 1540
  190.4 80.0 %copy-start.4 = (bf16[2,1,256,128]{3,2,1,0:T(8,128)(2,1)S(1)}, bf16[2,1,256,128]{3,2,1,0:T(8,128)(2,1)}, u32[]{:S(2)}) copy-start(bf16[2,1,256,128]{3,2,1,0:T(8,128)(2,1)} %param.15) | copy-start | bytes 393220
  264.4 33.1 %all-to-all-start.1 = ((bf16[4,16,9,1024]{3,1,2,0:T(8,128)(2,1)}), bf16[4,16,9,1024]{3,1,2,0:T(8,128)(2,1)S(1)}, u32[]{:S(2)}, u32[]{:S(2)}) async-start(bf16[4,16,9,1024]{3,1,2,0:T(8,128)(2,1)} %copy.59), calls=%async_computation.2 | async-start | bytes 2359296 | tf_op jit(solution)/shard_map/all_to_all | solution.py:87
Sparse Core Ops, SparseCore 0:
  190.6 70.4 reduce-scatter.1
where the time goes:
time: 310 us; the launch traced here: 309 us
  blocking collectives  118 us (38%)
  waiting for transfers between devices  96.1 us (31%)
  matrix products  49 us (16%)
  local copies, waits for them, and re-layouts  23.9 us (8%)
  between operations  14.2 us (5%)
  starting transfers between devices  4.65 us (2%)
  other arithmetic  3.3 us (1%)
    all_to_all x1, blocking collectives, on_device(): lax.all_to_all(sending, 'afd', split_axis=0, concat_axis=0, tiled=True)  110 us
    reduce_scatter x1, waiting for transfers between devices, on_device(): lax.psum_scatter(partial_value.astype(jnp.bfloat16), 'tp', scatter_dimens...  69.8 us
    all_to_all x1, waiting for transfers between devices, on_device(): lax.all_to_all(summed, 'afd', split_axis=0, concat_axis=0, tiled=True)  26.3 us
    dot_general x1, matrix products, on_device(): jnp.einsum('sncf,nfd->sncd', hidden, down_weight, preferred_element_type=...  16.2 us
    reshape x2, local copies, waits for them, and re-layouts, on_device(): sending = sending.reshape(owners, held_experts, CAP, whole_rows.shape[1])  14.3 us
    dot_general x1, matrix products, on_device(): jnp.einsum('snce,nef->sncf', received, up_weight, preferred_element_type=...  14 us
    dot_general x1, matrix products, on_device(): jnp.einsum('snce,nef->sncf', received, gate_weight, preferred_element_typ...  13.7 us
    all_gather x1, blocking collectives, on_device(): whole_rows = lax.all_gather(moe_in, 'tp', axis=1, tiled=True)  8.12 us
  transfers between devices with their start and end apart: 2, of which 2 were waited for; matrix products, arithmetic and copies ran while one was open for 1% of the time, Pallas kernels for 0%

commit v1 on v0

--- a/solution.py
+++ b/solution.py
@@ -6,7 +6,6 @@
 from jax.sharding import PartitionSpec as P
 
 EXPERTS = 64
-CAP = 9
 
 
 def attend(queries, cache_keys, cache_values, new_keys, new_values, cache_lengths):
@@ -40,13 +39,6 @@
     return mixed.reshape(requests, head_count, head_width).astype(jnp.bfloat16)
 
 
-def ranks(choice_ids):
-    flat_ids = choice_ids.reshape(-1)
-    matches = (flat_ids[:, None] == jnp.arange(EXPERTS, dtype=jnp.int32)[None, :]).astype(jnp.int32)
-    earlier = jnp.cumsum(matches, axis=0) - matches
-    return jnp.sum(earlier * matches, axis=1).reshape(choice_ids.shape)
-
-
 def on_device(
     queries,
     cache_keys,
@@ -63,36 +55,27 @@
     down_weight,
 ):
     attn_out = attend(queries, cache_keys, cache_values, new_keys, new_values, cache_lengths)
-    owners = lax.axis_size("afd")
     held_experts = gate_weight.shape[0]
-    slot_id = expert_ids * CAP + ranks(expert_ids)
-    slot_count = owners * held_experts * CAP
-    slot_index = jnp.arange(slot_count, dtype=jnp.int32)[:, None, None]
-    placing = jnp.any(slot_index == slot_id[None], axis=2).astype(jnp.bfloat16)
-    whole_rows = lax.all_gather(moe_in, "tp", axis=1, tiled=True)
-    sending = jnp.dot(placing, whole_rows, preferred_element_type=jnp.float32).astype(jnp.bfloat16)
-    sending = sending.reshape(owners, held_experts, CAP, whole_rows.shape[1])
-    received = lax.all_to_all(sending, "afd", split_axis=0, concat_axis=0, tiled=True)
-    gate_part = jnp.einsum(
-        "snce,nef->sncf", received, gate_weight, preferred_element_type=jnp.float32
-    )
-    up_part = jnp.einsum("snce,nef->sncf", received, up_weight, preferred_element_type=jnp.float32)
-    hidden = (jax.nn.silu(gate_part) * up_part).astype(jnp.bfloat16)
-    partial_value = jnp.einsum(
-        "sncf,nfd->sncd", hidden, down_weight, preferred_element_type=jnp.float32
-    )
-    summed = lax.psum_scatter(
-        partial_value.astype(jnp.bfloat16), "tp", scatter_dimension=3, tiled=True
-    )
-    answers = lax.all_to_all(summed, "afd", split_axis=0, concat_axis=0, tiled=True)
-    returned_rows = answers.reshape(slot_count, answers.shape[3])
-    picked = jnp.take(returned_rows, slot_id, axis=0).astype(jnp.float32)
+    owner = lax.axis_index("afd")
     table_hits = (
         gate_index[..., None] == jnp.arange(gate_table.shape[0], dtype=jnp.int32)[None, None, :]
     ).astype(jnp.float32)
     raw_gates = jnp.sum(table_hits * gate_table[None, None, :], axis=2)
     route_weight = raw_gates / jnp.sum(raw_gates, axis=1, keepdims=True)
-    moe_out = jnp.einsum("tk,tkd->td", route_weight, picked).astype(jnp.bfloat16)
+    chosen = expert_ids[..., None] == jnp.arange(EXPERTS, dtype=jnp.int32)
+    routing = jnp.sum(jnp.where(chosen, route_weight[..., None], 0.0), axis=1)
+    all_routing = lax.all_gather(routing, "afd", axis=0, tiled=True)
+    held_routing = lax.dynamic_slice_in_dim(all_routing, owner * held_experts, held_experts, axis=1)
+    all_rows = lax.all_gather(moe_in, "afd", axis=0, tiled=True)
+    all_rows = lax.all_gather(all_rows, "tp", axis=1, tiled=True)
+    gate_part = jnp.einsum("te,nef->tnf", all_rows, gate_weight, preferred_element_type=jnp.float32)
+    up_part = jnp.einsum("te,nef->tnf", all_rows, up_weight, preferred_element_type=jnp.float32)
+    hidden = jax.nn.silu(gate_part) * up_part
+    scaled = (hidden * held_routing[:, :, None]).astype(jnp.bfloat16)
+    partial_value = jnp.einsum("tnf,nfd->td", scaled, down_weight, preferred_element_type=jnp.float32)
+    partial_value = partial_value.astype(jnp.bfloat16)
+    summed = lax.psum_scatter(partial_value, "tp", scatter_dimension=1, tiled=True)
+    moe_out = lax.psum_scatter(summed, "afd", scatter_dimension=0, tiled=True)
     return (attn_out, moe_out)
 
 

time: 310 us -> 145 us (0.47)
  blocking collectives: 118 us -> 31.6 us
  waiting for transfers between devices: 96.1 us -> 53.3 us
  local copies, waits for them, and re-layouts: 23.9 us -> 1.73 us
  matrix products: 49 us -> 42.4 us
  starting transfers between devices: 4.65 us -> 0.12 us
    all_to_all x1 -> x0, blocking collectives: 110 us -> none  [on_device(): lax.all_to_all(sending, 'afd', split_axis=0, concat_axis=0, tiled=True)]
    all_to_all x1 -> x0, waiting for transfers between devices: 26.3 us -> none  [on_device(): lax.all_to_all(summed, 'afd', split_axis=0, concat_axis=0, tiled=True)]
    all_gather x1 -> x2, blocking collectives: 8.12 us -> 31.6 us  [the longest x1 18.4 us: on_device(): all_rows = lax.all_gather(moe_in, 'afd', axis=0, tiled=True)]
    reduce_scatter x1 -> x2, waiting for transfers between devices: 69.8 us -> 50.5 us  [the longest x1 27.9 us: on_device(): lax.psum_scatter(partial_value, 'tp', scatter_dimension=1, tiled=True)]
    reshape x5 -> x0, local copies, waits for them, and re-layouts: 15 us -> none  [the longest x2 14.3 us: on_device(): sending = sending.reshape(owners, held_experts, CAP, whole_rows.shape[1])]
    dot_general x5 -> x3, matrix products: 47.9 us -> 41.3 us  [the longest x1 16.4 us: on_device(): jnp.einsum('te,nef->tnf', all_rows, up_weight, preferred_element_type=jnp...]
    all_to_all x1 -> x0, starting transfers between devices: 4.61 us -> none  [on_device(): lax.all_to_all(summed, 'afd', split_axis=0, concat_axis=0, tiled=True)]
    reduce_scatter x1 -> x0, local copies, waits for them, and re-layouts: 3.33 us -> none  [on_device(): lax.psum_scatter(partial_value.astype(jnp.bfloat16), 'tp', scatter_dimens...]
  transfers between devices with their start and end apart: 2 -> 3, of which waited for: 2 -> 3; matrix products, arithmetic and copies ran while one was open for 1% -> 3% of each run, Pallas kernels for 0% -> 0%
where the time goes in v1:
time: 145 us
  waiting for transfers between devices  53.3 us (37%)
  matrix products  42.4 us (29%)
  blocking collectives  31.6 us (22%)
  between operations  13.9 us (10%)
  other arithmetic  1.97 us (1%)
  local copies, waits for them, and re-layouts  1.73 us (1%)
    reduce_scatter x1, waiting for transfers between devices, on_device(): lax.psum_scatter(partial_value, 'tp', scatter_dimension=1, tiled=True)  27.9 us
    reduce_scatter x1, waiting for transfers between devices, on_device(): moe_out = lax.psum_scatter(summed, 'afd', scatter_dimension=0, tiled=True)  22.6 us
    all_gather x1, blocking collectives, on_device(): all_rows = lax.all_gather(moe_in, 'afd', axis=0, tiled=True)  18.4 us
    dot_general x1, matrix products, on_device(): jnp.einsum('te,nef->tnf', all_rows, up_weight, preferred_element_type=jnp...  16.4 us
    all_gather x1, blocking collectives, on_device(): all_routing = lax.all_gather(routing, 'afd', axis=0, tiled=True)  13.2 us
    dot_general x1, matrix products, on_device(): jnp.einsum('te,nef->tnf', all_rows, gate_weight, preferred_element_type=j...  12.7 us
    dot_general x1, matrix products, on_device(): jnp.einsum('tnf,nfd->td', scaled, down_weight, preferred_element_type=jnp...  12.2 us
  transfers between devices with their start and end apart: 3, of which 3 were waited for; matrix products, arithmetic and copies ran while one was open for 3% of the time, Pallas kernels for 0%

profile of v1, /device:TPU:0, one launch (start us, length us, event | category | flops | bytes accessed | tf_op | source)
XLA Modules:
  0.0 145.0 jit_solution(12890326760648845823)
XLA Ops:
  7.2 0.0 copy-start
  7.2 0.0 all-gather.2.cloned.1.call-start
  7.2 18.4 %all_gather.9 = bf16[192,1024]{1,0:T(8,128)(2,1)} all-gather(bf16[48,1024]{1,0:T(8,128)(2,1)} %param.19), channel_id=1, replica_groups=mesh['groups'=2,'afd'=4,'tp'=4] {'afd'}, dimensions={0}, use_global_device_ids=true | all-gather | bytes 491520 | tf_op jit(solution)/shard_map/all_gather | solution.py:69
  25.6 0.0 all-gather.2.cloned.1.call-update
  25.6 0.0 reduce-scatter.3.cloned.1.call-start
  25.7 0.8 copy.20
  26.4 0.8 copy.21
  27.2 1.4 %select_reduce_fusion = (f32[48]{0:T(128)S(1)}, f32[48,8]{1,0:T(8,128)S(1)}) fusion(f32[256]{0:T(256)} %param.22, s32[48,8]{1,0:T(8,128)S(1)} %copy.21), kind=kLoop, calls=%fused_computation.12 | loop fusion | flops 392784 | bytes 4288 | tf_op jit(solution)/shard_map/reduce_sum | solution.py:64
  28.6 0.1 broadcast_divide_fusion
  28.7 0.2 select_reduce_fusion.2
  28.9 13.2 %all_gather.11 = f32[192,64]{1,0:T(8,128)S(1)} all-gather(f32[48,64]{1,0:T(8,128)S(1)} %select_reduce_fusion.2), channel_id=1, replica_groups=mesh['groups'=2,'afd'=4,'tp'=4] {'afd'}, dimensions={0}, use_global_device_ids=true | all-gather | bytes 61440 | tf_op jit(solution)/shard_map/all_gather | solution.py:67
  42.2 0.1 constant_dynamic-slice_fusion
  42.2 0.1 copy.22
  42.3 2.8 %all-gather.2.cloned.1.call-done = bf16[192,4096]{1,0:T(8,128)(2,1)} async-done(((bf16[192,1024]{1,0:T(8,128)(2,1)}), bf16[192,4096]{1,0:T(8,128)(2,1)}) %all-gather.2.cloned.1.call-update) | async-done | bytes 1572880 | tf_op jit(solution)/shard_map/all_gather | solution.py:70
  45.1 0.0 copy-start.2
  45.1 16.4 %fusion.1 = f32[192,16,192]{2,0,1:T(8,128)} fusion(bf16[16,4096,192]{1,2,0:T(8,128)(2,1)} %param.24, bf16[192,4096]{1,0:T(8,128)(2,1)} %all-gather.2.cloned.1.call-done), kind=kOutput, calls=%fused_computation.3 | convolution fusion | flops 4831838208 | bytes 29097984 | tf_op jit(solution)/shard_map/te,nef->tnf/dot_general | solution.py:72
  61.5 0.0 copy-done.2
  61.5 12.7 %multiply_convert_fusion.clone.4 = bf16[192,16,192]{2,0,1:T(8,128)(2,1)S(1)} fusion(f32[192,16,192]{2,0,1:T(8,128)} %fusion.1, bf16[16,4096,192]{1,2,0:T(8,128)(2,1)} %param.23, bf16[192,4096]{1,0:T(8,128)(2,1)S(1)} %copy-done.2, f32[192,16]{0,1:T(8,128)S(1)} %copy.22), kind=kOutput, calls=%fused_computation.2.clone.clone.clone.1 | convolution fusion | flops 4835966976 | bytes 30289920 | tf_op jit(solution)/shard_map/te,nef->tnf/dot_general | solution.py:71
  74.2 0.0 copy-start.4
  74.2 0.0 copy-start.1
  74.2 0.0 copy-start.5
  74.2 0.0 copy-start.6
  74.3 0.0 copy-start.3
  74.3 12.2 %fusion = bf16[192,4096]{1,0:T(8,128)(2,1)} fusion(bf16[16,192,4096]{2,1,0:T(8,128)(2,1)} %param.25, bf16[192,16,192]{2,0,1:T(8,128)(2,1)S(1)} %multiply_convert_fusion.clone.4), kind=kOutput, calls=%fused_computation.1 | convolution fusion | flops 4832624640 | bytes 27918336 | tf_op jit(solution)/shard_map/tnf,nfd->td/dot_general | solution.py:75
  86.5 0.0 reduce-scatter.3.cloned.1.call-update
  86.5 0.0 reduce-scatter.5.cloned.1.call-start
  86.6 0.0 copy-done.4
  86.6 0.1 iota_compare_fusion.2
  86.6 0.0 copy-done.1
  86.6 0.0 copy-done.5
  86.6 0.1 fusion.16
  86.8 0.0 copy-done
  86.8 0.2 fusion.22
  87.0 27.9 %reduce-scatter.3.cloned.1.call-done = bf16[192,1024]{1,0:T(8,128)(2,1)} async-done(((bf16[192,4096]{1,0:T(8,128)(2,1)}), bf16[192,1024]{1,0:T(8,128)(2,1)}) %reduce-scatter.3.cloned.1.call-update) | async-done | bytes 393232 | tf_op jit(solution)/shard_map/reduce_scatter | solution.py:77
  114.9 0.0 reduce-scatter.5.cloned.1.call-update
  114.9 0.2 fusion.11
  115.1 0.0 copy-done.6
  115.1 0.0 copy-done.3
  115.1 0.8 fusion.8
  115.9 22.6 %reduce-scatter.5.cloned.1.call-done = bf16[48,1024]{1,0:T(8,128)(2,1)} async-done(((bf16[192,1024]{1,0:T(8,128)(2,1)}), bf16[48,1024]{1,0:T(8,128)(2,1)}) %reduce-scatter.5.cloned.1.call-update) | async-done | bytes 98320 | tf_op jit(solution)/shard_map/reduce_scatter | solution.py:78
  (3 shorter events, 0.0 us)
Async XLA Ops:
  7.2 79.6 %copy-start = (bf16[2,1,256,128]{3,2,1,0:T(8,128)(2,1)S(1)}, bf16[2,1,256,128]{3,2,1,0:T(8,128)(2,1)}, u32[]{:S(2)}) copy-start(bf16[2,1,256,128]{3,2,1,0:T(8,128)(2,1)} %param.14) | copy-start | bytes 393220
  7.2 38.0 %all-gather.2.cloned.1.call-start = ((), (), s32[]{:S(2)}) async-start(), calls=%async_computation.2 | async-start | bytes 1966080 | tf_op jit(solution)/shard_map/all_gather | solution.py:70
  25.6 89.3 %reduce-scatter.3.cloned.1.call-start = ((), (), s32[]{:S(2)}) async-start(), calls=%async_computation.3 | async-start | bytes 1966080 | tf_op jit(solution)/shard_map/reduce_scatter | solution.py:77
  45.1 16.4 %copy-start.2 = (bf16[192,4096]{1,0:T(8,128)(2,1)S(1)}, bf16[192,4096]{1,0:T(8,128)(2,1)}, u32[]{:S(2)}) copy-start(bf16[192,4096]{1,0:T(8,128)(2,1)} %all-gather.2.cloned.1.call-done) | copy-start | bytes 4718596
  74.2 12.3 %copy-start.4 = (s32[2]{0:T(128)S(1)}, s32[2]{0:T(128)}, u32[]{:S(2)}) copy-start(s32[2]{0:T(128)} %param.18) | copy-start | bytes 28
  74.2 12.4 %copy-start.1 = (bf16[2,16,128]{2,1,0:T(8,128)(2,1)S(1)}, bf16[2,16,128]{2,1,0:T(8,128)(2,1)}, u32[]{:S(2)}) copy-start(bf16[2,16,128]{2,1,0:T(8,128)(2,1)} %param.13) | copy-start | bytes 24580
  74.2 12.4 %copy-start.5 = (bf16[2,1,128]{2,0,1:T(2,128)(2,1)S(1)}, bf16[2,1,128]{2,0,1:T(2,128)(2,1)}, u32[]{:S(2)}) copy-start(bf16[2,1,128]{2,0,1:T(2,128)(2,1)} %param.16) | copy-start | bytes 1540
  74.2 40.8 %copy-start.6 = (bf16[2,1,128]{2,0,1:T(2,128)(2,1)S(1)}, bf16[2,1,128]{2,0,1:T(2,128)(2,1)}, u32[]{:S(2)}) copy-start(bf16[2,1,128]{2,0,1:T(2,128)(2,1)} %param.17) | copy-start | bytes 1540
  74.3 40.8 %copy-start.3 = (bf16[2,1,256,128]{3,2,1,0:T(8,128)(2,1)S(1)}, bf16[2,1,256,128]{3,2,1,0:T(8,128)(2,1)}, u32[]{:S(2)}) copy-start(bf16[2,1,256,128]{3,2,1,0:T(8,128)(2,1)} %param.15) | copy-start | bytes 393220
  86.5 52.0 %reduce-scatter.5.cloned.1.call-start = ((), (), s32[]{:S(2)}) async-start(), calls=%async_computation.4 | async-start | bytes 491520 | tf_op jit(solution)/shard_map/reduce_scatter | solution.py:78
Sparse Core Ops, SparseCore 0:
  25.7 19.3 all-gather.1
  86.6 28.1 reduce-scatter.2
  117.8 20.5 reduce-scatter.4

commit v2 on v1

--- a/solution.py
+++ b/solution.py
@@ -1,11 +1,15 @@
+import functools
 import math
 
 import jax
 import jax.numpy as jnp
 from jax import lax
+from jax.experimental import pallas as pl
+from jax.experimental.pallas import tpu as pltpu
 from jax.sharding import PartitionSpec as P
 
 EXPERTS = 64
+SLOTS = 4
 
 
 def attend(queries, cache_keys, cache_values, new_keys, new_values, cache_lengths):
@@ -79,6 +83,435 @@
     return (attn_out, moe_out)
 
 
+def fused_kernel(
+    owners,
+    queries_ref,
+    keys_ref,
+    values_ref,
+    new_keys_ref,
+    new_values_ref,
+    lengths_ref,
+    rows_ref,
+    ids_ref,
+    index_ref,
+    table_ref,
+    gate_hbm,
+    up_hbm,
+    down_hbm,
+    attn_ref,
+    moe_ref,
+    gate_buf,
+    up_buf,
+    down_buf,
+    all_rows,
+    routing,
+    hidden,
+    part,
+    core_got,
+    x_got,
+    z_got,
+    gate_sem,
+    up_sem,
+    down_sem,
+    zg_send,
+    zg_recv,
+    rt_send,
+    rt_recv,
+    xg_send,
+    xg_recv,
+    cg_send,
+    cg_recv,
+    cs_send,
+    cs_recv,
+    xs_send,
+    xs_recv,
+    zs_send,
+    zs_recv,
+):
+    owner = lax.axis_index("afd")
+    mine = lax.axis_index("tp")
+    core_peer = mine + 1 - 2 * lax.rem(mine, 2)
+    x_peer = lax.rem(mine + 2, 4)
+    diagonal = lax.rem(core_peer + 2, 4)
+    tokens, width = rows_ref.shape
+    pairs = gate_hbm.shape[0] // 2
+    slots = gate_buf.shape[0]
+    ffe = gate_hbm.shape[1]
+    everyone = owners * tokens
+
+    def pair_copies(pair, slot):
+        experts = pl.ds(pair * 2, 2)
+        return (
+            pltpu.make_async_copy(gate_hbm.at[experts], gate_buf.at[slot], gate_sem.at[slot]),
+            pltpu.make_async_copy(up_hbm.at[experts], up_buf.at[slot], up_sem.at[slot]),
+        )
+
+    chunk_order = (diagonal, x_peer, core_peer, mine)
+
+    def down_copy(step):
+        columns = pl.ds(pl.multiple_of(chunk_order[step] * width, width), width)
+        return pltpu.make_async_copy(
+            down_hbm.at[:, :, columns], down_buf.at[step], down_sem.at[step]
+        )
+
+    def send(src, dst, send_sem, recv_sem, where):
+        return pltpu.make_async_remote_copy(
+            src_ref=src,
+            dst_ref=dst,
+            send_sem=send_sem,
+            recv_sem=recv_sem,
+            device_id=where,
+            device_id_type=pl.DeviceIdType.MESH,
+        )
+
+    barrier = pltpu.get_barrier_semaphore()
+    hops = sorted(range(1, owners), key=lambda j: min(j, owners - j))
+    peers = [{"afd": lax.rem(owner + j, owners)} for j in hops]
+    for where in peers + [{"tp": x_peer}, {"tp": core_peer}]:
+        pl.semaphore_signal(barrier, inc=1, device_id=where, device_id_type=pl.DeviceIdType.MESH)
+
+    for slot in range(slots):
+        for copy in pair_copies(slot, slot):
+            copy.start()
+    for step in range(4):
+        down_copy(step).start()
+
+    table = table_ref[...]
+    places = lax.broadcasted_iota(jnp.int32, (tokens, table.shape[1]), 1)
+    index = index_ref[...]
+    raw = [
+        jnp.sum(jnp.where(places == index[:, k : k + 1], table, 0.0), axis=1, keepdims=True)
+        for k in range(index.shape[1])
+    ]
+    total = sum(raw[1:], raw[0])
+    lanes = lax.broadcasted_iota(jnp.int32, (tokens, 128), 1)
+    ids = ids_ref[...]
+    placed = jnp.zeros((tokens, 128), jnp.float32)
+    for k in range(index.shape[1]):
+        placed = placed + jnp.where(lanes == ids[:, k : k + 1], raw[k] / total, 0.0)
+    routing[owner] = placed
+    all_rows[mine, owner] = rows_ref[...]
+
+    pl.semaphore_wait(barrier, owners - 1 + 2)
+
+    def z_gather(j, sender, target):
+        return send(
+            all_rows.at[mine, sender],
+            all_rows.at[mine, sender],
+            zg_send.at[j],
+            zg_recv.at[j],
+            {"afd": target},
+        )
+
+    def route_gather(j, sender, target):
+        return send(
+            routing.at[sender], routing.at[sender], rt_send.at[j], rt_recv.at[j], {"afd": target}
+        )
+
+    def x_gather(j, source):
+        return send(
+            all_rows.at[mine, source],
+            all_rows.at[mine, source],
+            xg_send.at[j],
+            xg_recv.at[j],
+            {"tp": x_peer},
+        )
+
+    def x_landed(j, source):
+        return send(
+            all_rows.at[x_peer, source],
+            all_rows.at[x_peer, source],
+            xg_send.at[j],
+            xg_recv.at[j],
+            {"tp": x_peer},
+        )
+
+    def core_gather(group, j, column, source):
+        return send(
+            all_rows.at[column, source],
+            all_rows.at[column, source],
+            cg_send.at[group, j],
+            cg_recv.at[group, j],
+            {"tp": core_peer},
+        )
+
+    for j in hops:
+        target = lax.rem(owner + j, owners)
+        z_gather(j, owner, target).start()
+    x_gather(0, owner).start()
+    core_gather(0, 0, mine, owner).start()
+    for j in hops:
+        route_gather(j, owner, lax.rem(owner + j, owners)).start()
+
+    requests, heads, head_width = queries_ref.shape
+    score_scale = 1.0 / math.sqrt(head_width)
+    for r in range(requests):
+        query = queries_ref[r]
+        scores = (
+            lax.dot_general(
+                query, keys_ref[r], (((1,), (1,)), ((), ())), preferred_element_type=jnp.float32
+            )
+            * score_scale
+        )
+        new_key = new_keys_ref[pl.ds(r, 1), :].astype(jnp.float32)
+        new_value = new_values_ref[pl.ds(r, 1), :].astype(jnp.float32)
+        fresh = (
+            jnp.sum(query.astype(jnp.float32) * new_key, axis=1, keepdims=True) * score_scale
+        )
+        positions = lax.broadcasted_iota(jnp.int32, scores.shape, 1)
+        valid = positions < lengths_ref[r]
+        masked = jnp.where(valid, scores, -jnp.inf)
+        largest = jnp.maximum(jnp.max(masked, axis=1, keepdims=True), fresh)
+        exp_scores = jnp.where(valid, jnp.exp(masked - largest), 0.0)
+        fresh_prob = jnp.exp(fresh - largest)
+        denominator = jnp.sum(exp_scores, axis=1, keepdims=True) + fresh_prob
+        weights = (exp_scores / denominator).astype(jnp.bfloat16)
+        fresh_weight = (fresh_prob / denominator).astype(jnp.bfloat16).astype(jnp.float32)
+        mixed = jnp.dot(weights, values_ref[r], preferred_element_type=jnp.float32)
+        attn_ref[r] = (mixed + fresh_weight * new_value).astype(jnp.bfloat16)
+
+    order = [0] + hops
+    for n, j in enumerate(order):
+        source = lax.rem(owner + owners - j, owners)
+        if j > 0:
+            z_gather(j, source, source).wait_recv()
+            x_gather(j, source).start()
+            core_gather(0, j, mine, source).start()
+        if n > 0:
+            before = order[n - 1]
+            source = lax.rem(owner + owners - before, owners)
+            x_landed(before, source).wait_recv()
+            core_gather(1, before, x_peer, source).start()
+    last = order[-1]
+    source = lax.rem(owner + owners - last, owners)
+    x_landed(last, source).wait_recv()
+    core_gather(1, last, x_peer, source).start()
+    for j in order:
+        source = lax.rem(owner + owners - j, owners)
+        if j > 0:
+            route_gather(j, source, source).wait_recv()
+        core_gather(0, j, core_peer, source).wait_recv()
+        core_gather(1, j, diagonal, source).wait_recv()
+    for j in order:
+        source = lax.rem(owner + owners - j, owners)
+        if j > 0:
+            z_gather(j, owner, source).wait_send()
+            route_gather(j, owner, source).wait_send()
+        x_gather(j, source).wait_send()
+        core_gather(0, j, mine, source).wait_send()
+        core_gather(1, j, x_peer, source).wait_send()
+
+    gates = routing[...].reshape(everyone, 128)
+    expert_lane = lax.broadcasted_iota(jnp.int32, (everyone, 128), 1)
+    unit = lax.broadcasted_iota(jnp.int32, (everyone, 2 * ffe), 1)
+
+    def pair_step(pair, carry):
+        slot = lax.rem(pair, slots)
+        for copy in pair_copies(pair, slot):
+            copy.wait()
+
+        def project(buf):
+            out = None
+            for t in range(4):
+                term = lax.dot_general(
+                    all_rows[t].reshape(everyone, width),
+                    buf[slot, :, :, t * width : (t + 1) * width].reshape(2 * ffe, width),
+                    (((1,), (1,)), ((), ())),
+                    preferred_element_type=jnp.float32,
+                )
+                out = term if out is None else out + term
+            return out
+
+        gate_part = project(gate_buf)
+        up_part = project(up_buf)
+        expert = owner * (2 * pairs) + 2 * pair
+        first = jnp.sum(jnp.where(expert_lane == expert, gates, 0.0), axis=1, keepdims=True)
+        second = jnp.sum(jnp.where(expert_lane == expert + 1, gates, 0.0), axis=1, keepdims=True)
+        scale = jnp.where(unit < ffe, first, second)
+        value = gate_part / (1.0 + jnp.exp(-gate_part)) * up_part * scale
+        hidden[pair] = value.astype(jnp.bfloat16)
+
+        @pl.when(pair + slots < pairs)
+        def _():
+            for copy in pair_copies(pair + slots, slot):
+                copy.start()
+
+        return carry
+
+    lax.fori_loop(0, pairs, pair_step, 0)
+
+    tile = 256
+
+    def down_step(step):
+        down_copy(step).wait()
+
+        def tile_step(n, carry):
+            columns = pl.ds(pl.multiple_of(n * tile, tile), tile)
+            out = None
+            for quad in range(pairs // 2):
+                left = jnp.concatenate([hidden[2 * quad], hidden[2 * quad + 1]], axis=1)
+                right = down_buf[step, 4 * quad : 4 * quad + 4, :, columns]
+                term = jnp.dot(
+                    left, right.reshape(4 * ffe, tile), preferred_element_type=jnp.float32
+                )
+                out = term if out is None else out + term
+            part[step, :, :, columns] = out.astype(jnp.bfloat16).reshape(owners, tokens, tile)
+            return carry
+
+        lax.fori_loop(0, width // tile, tile_step, 0)
+
+    def core_send(k, step):
+        return send(
+            part.at[step], core_got.at[k], cs_send.at[k], cs_recv.at[k], {"tp": core_peer}
+        )
+
+    def x_send(j, piece):
+        return send(
+            part.at[1, piece], x_got.at[piece], xs_send.at[j], xs_recv.at[j], {"tp": x_peer}
+        )
+
+    def z_send(j, piece):
+        return send(
+            part.at[3, piece], z_got.at[j], zs_send.at[j], zs_recv.at[j], {"afd": piece}
+        )
+
+    def add_in(step, piece, got):
+        part[step, piece] = (
+            part[step, piece].astype(jnp.float32) + got.astype(jnp.float32)
+        ).astype(jnp.bfloat16)
+
+    far_first = hops[::-1] + [0]
+    down_step(0)
+    core_send(0, 0).start()
+    down_step(1)
+    core_send(0, 0).wait_recv()
+    for j in far_first:
+        piece = lax.rem(owner + j, owners)
+        add_in(1, piece, core_got[0, piece])
+        x_send(j, piece).start()
+    down_step(2)
+    core_send(1, 2).start()
+    down_step(3)
+    core_send(1, 2).wait_recv()
+    for j in far_first:
+        piece = lax.rem(owner + j, owners)
+        x_send(j, piece).wait_recv()
+        part[3, piece] = (
+            part[3, piece].astype(jnp.float32)
+            + core_got[1, piece].astype(jnp.float32)
+            + x_got[piece].astype(jnp.float32)
+        ).astype(jnp.bfloat16)
+        if j > 0:
+            z_send(j, piece).start()
+    result = part[3, owner].astype(jnp.float32)
+    for j in hops:
+        z_send(j, lax.rem(owner + j, owners)).wait_recv()
+        result = result + z_got[j].astype(jnp.float32)
+    moe_ref[...] = result.astype(jnp.bfloat16)
+    core_send(0, 0).wait_send()
+    core_send(1, 2).wait_send()
+    for j in far_first:
+        piece = lax.rem(owner + j, owners)
+        x_send(j, piece).wait_send()
+        if j > 0:
+            z_send(j, piece).wait_send()
+
+
+def fused(
+    queries,
+    cache_keys,
+    cache_values,
+    new_keys,
+    new_values,
+    cache_lengths,
+    moe_in,
+    expert_ids,
+    gate_index,
+    gate_table,
+    gate_weight,
+    up_weight,
+    down_weight,
+):
+    owners = lax.axis_size("afd")
+    tokens, width = moe_in.shape
+    held, ffe, full = down_weight.shape
+    requests, _, cached, head_width = cache_keys.shape
+    vmem = pl.BlockSpec(memory_space=pltpu.VMEM)
+    smem = pl.BlockSpec(memory_space=pltpu.SMEM)
+    hbm = pl.BlockSpec(memory_space=pl.ANY)
+    slots = min(SLOTS, held // 2)
+    dma = pltpu.SemaphoreType.DMA
+    bf16 = jnp.bfloat16
+    return pl.pallas_call(
+        functools.partial(fused_kernel, owners),
+        out_shape=(
+            jax.ShapeDtypeStruct(queries.shape, bf16),
+            jax.ShapeDtypeStruct(moe_in.shape, bf16),
+        ),
+        in_specs=[vmem] * 5 + [smem] + [vmem] * 4 + [hbm] * 3,
+        out_specs=(vmem, vmem),
+        scratch_shapes=[
+            pltpu.VMEM((slots, 2, ffe, full), bf16),
+            pltpu.VMEM((slots, 2, ffe, full), bf16),
+            pltpu.VMEM((4, held, ffe, width), bf16),
+            pltpu.VMEM((4, owners, tokens, width), bf16),
+            pltpu.VMEM((owners, tokens, 128), jnp.float32),
+            pltpu.VMEM((held // 2, owners * tokens, 2 * ffe), bf16),
+            pltpu.VMEM((4, owners, tokens, width), bf16),
+            pltpu.VMEM((2, owners, tokens, width), bf16),
+            pltpu.VMEM((owners, tokens, width), bf16),
+            pltpu.VMEM((owners, tokens, width), bf16),
+            dma((slots,)),
+            dma((slots,)),
+            dma((4,)),
+            dma((owners,)),
+            dma((owners,)),
+            dma((owners,)),
+            dma((owners,)),
+            dma((owners,)),
+            dma((owners,)),
+            dma((2, owners)),
+            dma((2, owners)),
+            dma((2,)),
+            dma((2,)),
+            dma((owners,)),
+            dma((owners,)),
+            dma((owners,)),
+            dma((owners,)),
+        ],
+        compiler_params=pltpu.CompilerParams(
+            collective_id=0, has_side_effects=True, vmem_limit_bytes=62 * 1024 * 1024
+        ),
+        cost_estimate=pl.CostEstimate(
+            flops=6 * held * owners * tokens * full * ffe,
+            bytes_accessed=6 * held * full * ffe,
+            transcendentals=held * owners * tokens * ffe,
+        ),
+    )(
+        queries,
+        cache_keys.reshape(requests, cached, head_width),
+        cache_values.reshape(requests, cached, head_width),
+        new_keys.reshape(requests, head_width),
+        new_values.reshape(requests, head_width),
+        cache_lengths,
+        moe_in,
+        expert_ids,
+        gate_index,
+        gate_table.reshape(1, -1),
+        jnp.swapaxes(gate_weight, 1, 2),
+        jnp.swapaxes(up_weight, 1, 2),
+        down_weight,
+    )
+
+
+def either(*args):
+    moe_in, gate_weight = args[6], args[10]
+    few_rows = lax.axis_size("afd") * moe_in.shape[0] <= 256
+    if few_rows and lax.axis_size("tp") == 4 and gate_weight.shape[0] % 4 == 0:
+        return fused(*args)
+    return on_device(*args)
+
+
 def solution(mesh):
     placed = (
         P(("groups", "afd"), "tp", None),
@@ -96,7 +529,7 @@
         P("afd", "tp", None),
     )
     return jax.shard_map(
-        on_device,
+        either,
         mesh=mesh,
         in_specs=placed,
         out_specs=(P(("groups", "afd"), "tp", None), P(("groups", "afd"), "tp")),

time: 145 us -> 65.9 us (0.45)
  Pallas kernels: 0 us -> 59.4 us
  waiting for transfers between devices: 53.3 us -> 0 us
  matrix products: 42.4 us -> 0 us
  blocking collectives: 31.6 us -> 0 us
  between operations: 13.9 us -> 0.64 us
  local copies, waits for them, and re-layouts: 1.73 us -> 5.58 us
  other arithmetic: 1.97 us -> 0 us
    pallas_call x0 -> x1, Pallas kernels: none -> 59.4 us  [fused(): pl.pallas_call(functools.partial(fused_kernel, owners), out_shape=(jax.Sh...]
    reduce_scatter x2 -> x0, waiting for transfers between devices: 50.5 us -> none  [the longest x1 27.9 us: on_device(): lax.psum_scatter(partial_value, 'tp', scatter_dimension=1, tiled=True)]
    dot_general x6 -> x0, matrix products: 42.4 us -> none  [the longest x1 16.4 us: on_device(): jnp.einsum('te,nef->tnf', all_rows, up_weight, preferred_element_type=jnp...]
    all_gather x2 -> x0, blocking collectives: 31.6 us -> none  [the longest x1 18.4 us: on_device(): all_rows = lax.all_gather(moe_in, 'afd', axis=0, tiled=True)]
    unnamed x16 -> x4, local copies, waits for them, and re-layouts: 1.58 us -> 5.58 us
    all_gather x1 -> x0, waiting for transfers between devices: 2.83 us -> none  [on_device(): all_rows = lax.all_gather(all_rows, 'tp', axis=1, tiled=True)]
    reduce_sum x3 -> x0, other arithmetic: 1.79 us -> none  [the longest x1 1.45 us: on_device(): route_weight = raw_gates / jnp.sum(raw_gates, axis=1, keepdims=True)]
  transfers between devices with their start and end apart: 3 -> 0, of which waited for: 3 -> 0; matrix products, arithmetic and copies ran while one was open for 3% -> 0% of each run, Pallas kernels for 0% -> 0%
where the time goes in v2:
time: 65.9 us; the launch traced here: 65.6 us
  Pallas kernels  59.4 us (90%)
  local copies, waits for them, and re-layouts  5.58 us (8%)
    pallas_call x1, Pallas kernels, fused(): pl.pallas_call(functools.partial(fused_kernel, owners), out_shape=(jax.Sh...  59.4 us
    unnamed x4, local copies, waits for them, and re-layouts  5.58 us

profile of v2, /device:TPU:0, one launch (start us, length us, event | category | flops | bytes accessed | tf_op | source)
XLA Modules:
  0.0 65.6 jit_solution(18040057169519046078)
XLA Ops:
  0.6 1.4 %copy.15.ids_ref = s32[48,8]{1,0:T(8,128)} copy(s32[48,8]{0,1:T(8,128)} %param.20) | data formatting | bytes 3072 | tf_op args[7]
  2.0 1.4 %copy.16.index_ref = s32[48,8]{1,0:T(8,128)} copy(s32[48,8]{0,1:T(8,128)} %param.21) | data formatting | bytes 3072 | tf_op args[8]
  3.4 59.4 %shard_map.140 = (bf16[2,16,128]{2,1,0:T(8,128)(2,1)}, bf16[48,1024]{1,0:T(8,128)(2,1)}) custom-call(bf16[2,16,128]{2,1,0:T(8,128)(2,1)} %queries_ref.1, bf16[2,256,128]{2,1,0:T(8,128)(2,1)} %bitcast.9, bf16[2,256,128]{2,1,0:T(8,128)(2,1)} %bitcast.10, bf16[2,128]{1,0:T(2,128)(2,1)} %bitcast.12, bf16[2,128]{1,0:T(2,128)(2,1)} %bitcast.13, s32[2]{0:T(128)} %lengths_ref.1, ...), custom_call_target="tpu_custom_call" | custom-call | flops 14495514624 | bytes 75497472 | tf_op jit(solution)/shard_map/pallas_call | solution.py:445
  62.8 1.3 %copy.19 = bf16[2,16,128]{2,1,0:T(8,128)(2,1)} copy(bf16[2,16,128]{2,1,0:T(8,128)(2,1)} %get-tuple-element.4) | data formatting | bytes 16384
  64.1 1.5 %copy.20 = bf16[48,1024]{1,0:T(8,128)(2,1)} copy(bf16[48,1024]{1,0:T(8,128)(2,1)} %get-tuple-element.5) | data formatting | bytes 196608

commit v3 on v2

--- a/solution.py
+++ b/solution.py
@@ -9,7 +9,8 @@
 from jax.sharding import PartitionSpec as P
 
 EXPERTS = 64
-SLOTS = 4
+SLOTS = 2
+GROUP = 4
 
 
 def attend(queries, cache_keys, cache_values, new_keys, new_values, cache_lengths):
@@ -134,13 +135,13 @@
     x_peer = lax.rem(mine + 2, 4)
     diagonal = lax.rem(core_peer + 2, 4)
     tokens, width = rows_ref.shape
-    pairs = gate_hbm.shape[0] // 2
+    groups = gate_hbm.shape[0] // GROUP
     slots = gate_buf.shape[0]
     ffe = gate_hbm.shape[1]
     everyone = owners * tokens
 
-    def pair_copies(pair, slot):
-        experts = pl.ds(pair * 2, 2)
+    def group_copies(group, slot):
+        experts = pl.ds(group * GROUP, GROUP)
         return (
             pltpu.make_async_copy(gate_hbm.at[experts], gate_buf.at[slot], gate_sem.at[slot]),
             pltpu.make_async_copy(up_hbm.at[experts], up_buf.at[slot], up_sem.at[slot]),
@@ -171,21 +172,21 @@
         pl.semaphore_signal(barrier, inc=1, device_id=where, device_id_type=pl.DeviceIdType.MESH)
 
     for slot in range(slots):
-        for copy in pair_copies(slot, slot):
+        for copy in group_copies(slot, slot):
             copy.start()
     for step in range(4):
         down_copy(step).start()
 
     table = table_ref[...]
     places = lax.broadcasted_iota(jnp.int32, (tokens, table.shape[1]), 1)
-    index = index_ref[...]
+    index = index_ref[...].T
     raw = [
         jnp.sum(jnp.where(places == index[:, k : k + 1], table, 0.0), axis=1, keepdims=True)
         for k in range(index.shape[1])
     ]
     total = sum(raw[1:], raw[0])
     lanes = lax.broadcasted_iota(jnp.int32, (tokens, 128), 1)
-    ids = ids_ref[...]
+    ids = ids_ref[...].T
     placed = jnp.zeros((tokens, 128), jnp.float32)
     for k in range(index.shape[1]):
         placed = placed + jnp.where(lanes == ids[:, k : k + 1], raw[k] / total, 0.0)
@@ -303,11 +304,11 @@
 
     gates = routing[...].reshape(everyone, 128)
     expert_lane = lax.broadcasted_iota(jnp.int32, (everyone, 128), 1)
-    unit = lax.broadcasted_iota(jnp.int32, (everyone, 2 * ffe), 1)
-
-    def pair_step(pair, carry):
-        slot = lax.rem(pair, slots)
-        for copy in pair_copies(pair, slot):
+    unit = lax.broadcasted_iota(jnp.int32, (everyone, GROUP * ffe), 1)
+
+    def group_step(group, carry):
+        slot = lax.rem(group, slots)
+        for copy in group_copies(group, slot):
             copy.wait()
 
         def project(buf):
@@ -315,7 +316,7 @@
             for t in range(4):
                 term = lax.dot_general(
                     all_rows[t].reshape(everyone, width),
-                    buf[slot, :, :, t * width : (t + 1) * width].reshape(2 * ffe, width),
+                    buf[slot, :, :, t * width : (t + 1) * width].reshape(GROUP * ffe, width),
                     (((1,), (1,)), ((), ())),
                     preferred_element_type=jnp.float32,
                 )
@@ -324,21 +325,24 @@
 
         gate_part = project(gate_buf)
         up_part = project(up_buf)
-        expert = owner * (2 * pairs) + 2 * pair
-        first = jnp.sum(jnp.where(expert_lane == expert, gates, 0.0), axis=1, keepdims=True)
-        second = jnp.sum(jnp.where(expert_lane == expert + 1, gates, 0.0), axis=1, keepdims=True)
-        scale = jnp.where(unit < ffe, first, second)
+        expert = GROUP * (owner * groups + group)
+        scale = None
+        for n in range(GROUP):
+            column = jnp.sum(
+                jnp.where(expert_lane == expert + n, gates, 0.0), axis=1, keepdims=True
+            )
+            scale = column if scale is None else jnp.where(unit < n * ffe, scale, column)
         value = gate_part / (1.0 + jnp.exp(-gate_part)) * up_part * scale
-        hidden[pair] = value.astype(jnp.bfloat16)
-
-        @pl.when(pair + slots < pairs)
+        hidden[group] = value.astype(jnp.bfloat16)
+
+        @pl.when(group + slots < groups)
         def _():
-            for copy in pair_copies(pair + slots, slot):
+            for copy in group_copies(group + slots, slot):
                 copy.start()
 
         return carry
 
-    lax.fori_loop(0, pairs, pair_step, 0)
+    lax.fori_loop(0, groups, group_step, 0)
 
     tile = 256
 
@@ -348,11 +352,12 @@
         def tile_step(n, carry):
             columns = pl.ds(pl.multiple_of(n * tile, tile), tile)
             out = None
-            for quad in range(pairs // 2):
-                left = jnp.concatenate([hidden[2 * quad], hidden[2 * quad + 1]], axis=1)
-                right = down_buf[step, 4 * quad : 4 * quad + 4, :, columns]
+            for group in range(groups):
+                right = down_buf[step, GROUP * group : GROUP * (group + 1), :, columns]
                 term = jnp.dot(
-                    left, right.reshape(4 * ffe, tile), preferred_element_type=jnp.float32
+                    hidden[group],
+                    right.reshape(GROUP * ffe, tile),
+                    preferred_element_type=jnp.float32,
                 )
                 out = term if out is None else out + term
             part[step, :, :, columns] = out.astype(jnp.bfloat16).reshape(owners, tokens, tile)
@@ -439,7 +444,7 @@
     vmem = pl.BlockSpec(memory_space=pltpu.VMEM)
     smem = pl.BlockSpec(memory_space=pltpu.SMEM)
     hbm = pl.BlockSpec(memory_space=pl.ANY)
-    slots = min(SLOTS, held // 2)
+    slots = min(SLOTS, held // GROUP)
     dma = pltpu.SemaphoreType.DMA
     bf16 = jnp.bfloat16
     return pl.pallas_call(
@@ -451,12 +456,12 @@
         in_specs=[vmem] * 5 + [smem] + [vmem] * 4 + [hbm] * 3,
         out_specs=(vmem, vmem),
         scratch_shapes=[
-            pltpu.VMEM((slots, 2, ffe, full), bf16),
-            pltpu.VMEM((slots, 2, ffe, full), bf16),
+            pltpu.VMEM((slots, GROUP, ffe, full), bf16),
+            pltpu.VMEM((slots, GROUP, ffe, full), bf16),
             pltpu.VMEM((4, held, ffe, width), bf16),
             pltpu.VMEM((4, owners, tokens, width), bf16),
             pltpu.VMEM((owners, tokens, 128), jnp.float32),
-            pltpu.VMEM((held // 2, owners * tokens, 2 * ffe), bf16),
+            pltpu.VMEM((held // GROUP, owners * tokens, GROUP * ffe), bf16),
             pltpu.VMEM((4, owners, tokens, width), bf16),
             pltpu.VMEM((2, owners, tokens, width), bf16),
             pltpu.VMEM((owners, tokens, width), bf16),
@@ -495,8 +500,8 @@
         new_values.reshape(requests, head_width),
         cache_lengths,
         moe_in,
-        expert_ids,
-        gate_index,
+        expert_ids.T,
+        gate_index.T,
         gate_table.reshape(1, -1),
         jnp.swapaxes(gate_weight, 1, 2),
         jnp.swapaxes(up_weight, 1, 2),
@@ -507,7 +512,7 @@
 def either(*args):
     moe_in, gate_weight = args[6], args[10]
     few_rows = lax.axis_size("afd") * moe_in.shape[0] <= 256
-    if few_rows and lax.axis_size("tp") == 4 and gate_weight.shape[0] % 4 == 0:
+    if few_rows and lax.axis_size("tp") == 4 and gate_weight.shape[0] % GROUP == 0:
         return fused(*args)
     return on_device(*args)
 

time: 65.9 us -> 62.7 us (0.951)
  local copies, waits for them, and re-layouts: 5.58 us -> 2.83 us
    unnamed x4 -> x2, local copies, waits for them, and re-layouts: 5.58 us -> 2.83 us
where the time goes in v3:
time: 62.7 us; the launch traced here: 62.5 us
  Pallas kernels  59 us (94%)
  local copies, waits for them, and re-layouts  2.83 us (5%)
  between operations  0.64 us (1%)
    pallas_call x1, Pallas kernels, fused(): pl.pallas_call(functools.partial(fused_kernel, owners), out_shape=(jax.Sh...  59 us
    unnamed x2, local copies, waits for them, and re-layouts  2.83 us

profile of v3, /device:TPU:0, one launch (start us, length us, event | category | flops | bytes accessed | tf_op | source)
XLA Modules:
  0.0 62.5 jit_solution(16946206676549255456)
XLA Ops:
  0.6 59.0 %shard_map.140 = (bf16[2,16,128]{2,1,0:T(8,128)(2,1)}, bf16[48,1024]{1,0:T(8,128)(2,1)}) custom-call(bf16[2,16,128]{2,1,0:T(8,128)(2,1)} %queries_ref.1, bf16[2,256,128]{2,1,0:T(8,128)(2,1)} %bitcast.11, bf16[2,256,128]{2,1,0:T(8,128)(2,1)} %bitcast.12, bf16[2,128]{1,0:T(2,128)(2,1)} %bitcast.16, bf16[2,128]{1,0:T(2,128)(2,1)} %bitcast.17, s32[2]{0:T(128)} %lengths_ref.1, ...), custom_call_target="tpu_custom_call" | custom-call | flops 14495514624 | bytes 75497472 | tf_op jit(solution)/shard_map/pallas_call | solution.py:450
  59.7 1.3 %copy.17 = bf16[2,16,128]{2,1,0:T(8,128)(2,1)} copy(bf16[2,16,128]{2,1,0:T(8,128)(2,1)} %get-tuple-element.4) | data formatting | bytes 16384
  61.0 1.5 %copy.18 = bf16[48,1024]{1,0:T(8,128)(2,1)} copy(bf16[48,1024]{1,0:T(8,128)(2,1)} %get-tuple-element.5) | data formatting | bytes 196608

commit v4 on v3

--- a/solution.py
+++ b/solution.py
@@ -293,15 +293,6 @@
             route_gather(j, source, source).wait_recv()
         core_gather(0, j, core_peer, source).wait_recv()
         core_gather(1, j, diagonal, source).wait_recv()
-    for j in order:
-        source = lax.rem(owner + owners - j, owners)
-        if j > 0:
-            z_gather(j, owner, source).wait_send()
-            route_gather(j, owner, source).wait_send()
-        x_gather(j, source).wait_send()
-        core_gather(0, j, mine, source).wait_send()
-        core_gather(1, j, x_peer, source).wait_send()
-
     gates = routing[...].reshape(everyone, 128)
     expert_lane = lax.broadcasted_iota(jnp.int32, (everyone, 128), 1)
     unit = lax.broadcasted_iota(jnp.int32, (everyone, GROUP * ffe), 1)
@@ -365,9 +356,14 @@
 
         lax.fori_loop(0, width // tile, tile_step, 0)
 
-    def core_send(k, step):
-        return send(
-            part.at[step], core_got.at[k], cs_send.at[k], cs_recv.at[k], {"tp": core_peer}
+    def core_send(k, step, j):
+        piece = lax.rem(owner + j, owners)
+        return send(
+            part.at[step, piece],
+            core_got.at[k, piece],
+            cs_send.at[k, j],
+            cs_recv.at[k, j],
+            {"tp": core_peer},
         )
 
     def x_send(j, piece):
@@ -387,19 +383,21 @@
 
     far_first = hops[::-1] + [0]
     down_step(0)
-    core_send(0, 0).start()
+    for j in far_first:
+        core_send(0, 0, j).start()
     down_step(1)
-    core_send(0, 0).wait_recv()
     for j in far_first:
         piece = lax.rem(owner + j, owners)
+        core_send(0, 0, j).wait_recv()
         add_in(1, piece, core_got[0, piece])
         x_send(j, piece).start()
     down_step(2)
-    core_send(1, 2).start()
+    for j in far_first:
+        core_send(1, 2, j).start()
     down_step(3)
-    core_send(1, 2).wait_recv()
     for j in far_first:
         piece = lax.rem(owner + j, owners)
+        core_send(1, 2, j).wait_recv()
         x_send(j, piece).wait_recv()
         part[3, piece] = (
             part[3, piece].astype(jnp.float32)
@@ -413,13 +411,21 @@
         z_send(j, lax.rem(owner + j, owners)).wait_recv()
         result = result + z_got[j].astype(jnp.float32)
     moe_ref[...] = result.astype(jnp.bfloat16)
-    core_send(0, 0).wait_send()
-    core_send(1, 2).wait_send()
     for j in far_first:
         piece = lax.rem(owner + j, owners)
+        core_send(0, 0, j).wait_send()
+        core_send(1, 2, j).wait_send()
         x_send(j, piece).wait_send()
         if j > 0:
             z_send(j, piece).wait_send()
+    for j in order:
+        source = lax.rem(owner + owners - j, owners)
+        if j > 0:
+            z_gather(j, owner, source).wait_send()
+            route_gather(j, owner, source).wait_send()
+        x_gather(j, source).wait_send()
+        core_gather(0, j, mine, source).wait_send()
+        core_gather(1, j, x_peer, source).wait_send()
 
 
 def fused(
@@ -477,8 +483,8 @@
             dma((owners,)),
             dma((2, owners)),
             dma((2, owners)),
-            dma((2,)),
-            dma((2,)),
+            dma((2, owners)),
+            dma((2, owners)),
             dma((owners,)),
             dma((owners,)),
             dma((owners,)),

time: 62.7 us -> 62.4 us (level)
  no operation moved by 1% of the time
where the time goes in v4:
time: 62.4 us; the launch traced here: 62.2 us
  Pallas kernels  58.7 us (94%)
  local copies, waits for them, and re-layouts  2.83 us (5%)
  between operations  0.64 us (1%)
    pallas_call x1, Pallas kernels, fused(): pl.pallas_call(functools.partial(fused_kernel, owners), out_shape=(jax.Sh...  58.7 us
    unnamed x2, local copies, waits for them, and re-layouts  2.83 us

profile of v4, /device:TPU:0, one launch (start us, length us, event | category | flops | bytes accessed | tf_op | source)
XLA Modules:
  0.0 62.2 jit_solution(2651515592274676723)
XLA Ops:
  0.6 58.7 %shard_map.140 = (bf16[2,16,128]{2,1,0:T(8,128)(2,1)}, bf16[48,1024]{1,0:T(8,128)(2,1)}) custom-call(bf16[2,16,128]{2,1,0:T(8,128)(2,1)} %queries_ref.1, bf16[2,256,128]{2,1,0:T(8,128)(2,1)} %bitcast.11, bf16[2,256,128]{2,1,0:T(8,128)(2,1)} %bitcast.12, bf16[2,128]{1,0:T(2,128)(2,1)} %bitcast.16, bf16[2,128]{1,0:T(2,128)(2,1)} %bitcast.17, s32[2]{0:T(128)} %lengths_ref.1, ...), custom_call_target="tpu_custom_call" | custom-call | flops 14495514624 | bytes 75497472 | tf_op jit(solution)/shard_map/pallas_call | solution.py:456
  59.4 1.3 %copy.17 = bf16[2,16,128]{2,1,0:T(8,128)(2,1)} copy(bf16[2,16,128]{2,1,0:T(8,128)(2,1)} %get-tuple-element.4) | data formatting | bytes 16384
  60.7 1.5 %copy.18 = bf16[48,1024]{1,0:T(8,128)(2,1)} copy(bf16[48,1024]{1,0:T(8,128)(2,1)} %get-tuple-element.5) | data formatting | bytes 196608

commit v5 on v4

--- a/solution.py
+++ b/solution.py
@@ -303,16 +303,12 @@
             copy.wait()
 
         def project(buf):
-            out = None
-            for t in range(4):
-                term = lax.dot_general(
-                    all_rows[t].reshape(everyone, width),
-                    buf[slot, :, :, t * width : (t + 1) * width].reshape(GROUP * ffe, width),
-                    (((1,), (1,)), ((), ())),
-                    preferred_element_type=jnp.float32,
-                )
-                out = term if out is None else out + term
-            return out
+            return lax.dot_general(
+                jnp.concatenate([all_rows[t].reshape(everyone, width) for t in range(4)], axis=1),
+                buf[slot].reshape(GROUP * ffe, 4 * width),
+                (((1,), (1,)), ((), ())),
+                preferred_element_type=jnp.float32,
+            )
 
         gate_part = project(gate_buf)
         up_part = project(up_buf)

time: 62.4 us -> 62.3 us (level)
  no operation moved by 1% of the time
where the time goes in v5:
time: 62.3 us; the launch traced here: 62.1 us
  Pallas kernels  58.6 us (94%)
  local copies, waits for them, and re-layouts  2.83 us (5%)
  between operations  0.64 us (1%)
    pallas_call x1, Pallas kernels, fused(): pl.pallas_call(functools.partial(fused_kernel, owners), out_shape=(jax.Sh...  58.6 us
    unnamed x2, local copies, waits for them, and re-layouts  2.83 us

profile of v5, /device:TPU:0, one launch (start us, length us, event | category | flops | bytes accessed | tf_op | source)
XLA Modules:
  0.0 62.1 jit_solution(11455280901362276432)
XLA Ops:
  0.6 58.6 %shard_map.140 = (bf16[2,16,128]{2,1,0:T(8,128)(2,1)}, bf16[48,1024]{1,0:T(8,128)(2,1)}) custom-call(bf16[2,16,128]{2,1,0:T(8,128)(2,1)} %queries_ref.1, bf16[2,256,128]{2,1,0:T(8,128)(2,1)} %bitcast.11, bf16[2,256,128]{2,1,0:T(8,128)(2,1)} %bitcast.12, bf16[2,128]{1,0:T(2,128)(2,1)} %bitcast.16, bf16[2,128]{1,0:T(2,128)(2,1)} %bitcast.17, s32[2]{0:T(128)} %lengths_ref.1, ...), custom_call_target="tpu_custom_call" | custom-call | flops 14495514624 | bytes 75497472 | tf_op jit(solution)/shard_map/pallas_call | solution.py:452
  59.2 1.3 %copy.17 = bf16[2,16,128]{2,1,0:T(8,128)(2,1)} copy(bf16[2,16,128]{2,1,0:T(8,128)(2,1)} %get-tuple-element.4) | data formatting | bytes 16384
  60.5 1.5 %copy.18 = bf16[48,1024]{1,0:T(8,128)(2,1)} copy(bf16[48,1024]{1,0:T(8,128)(2,1)} %get-tuple-element.5) | data formatting | bytes 196608
